TPU v7x, 128 devices: a whole 4x4x4 slice. The times are simulated.
128 devices in a mesh: gossip: 8 (over x, z_hi), fsdp: 2 (over z_lo), tensor: 8 (over y, core).
Axes of the slice: x: 4, y: 4, z: 4 (z_hi: 2, z_lo: 2; z = z_hi * 2 + z_lo), core: 2. Of those that a mesh axis runs over, the one named last changes fastest.
Arguments:
- normed: bfloat16 [8192, 8192], P(('gossip', 'fsdp', 'tensor')), may hold values from -24 to 24
- key_cotangent: bfloat16 [8192, 1024], P(('gossip', 'fsdp'), 'tensor'), may hold values from -6 to 6
- value_cotangent: bfloat16 [8192, 1024], P(('gossip', 'fsdp'), 'tensor'), may hold values from -6 to 6
- key_weight: float32 [8, 8192, 1024], P('gossip', 'fsdp', 'tensor'), may hold values from -6 to 6
- value_weight: float32 [8, 8192, 1024], P('gossip', 'fsdp', 'tensor'), may hold values from -6 to 6
- key_momentum: float32 [8, 8192, 1024], P('gossip', 'fsdp', 'tensor'), may hold values from -6 to 6
- value_momentum: float32 [8, 8192, 1024], P('gossip', 'fsdp', 'tensor'), may hold values from -6 to 6
- step_index: int32 [], replicated, may hold values from 0 to 2999
Outputs:
- projected_keys: bfloat16 [8192, 1024], P(('gossip', 'fsdp'), 'tensor')
- projected_values: bfloat16 [8192, 1024], P(('gossip', 'fsdp'), 'tensor')
- input_grad: bfloat16 [8192, 8192], P(('gossip', 'fsdp', 'tensor'))
- new_key_weight: float32 [8, 8192, 1024], P('gossip', 'fsdp', 'tensor')
- new_value_weight: float32 [8, 8192, 1024], P('gossip', 'fsdp', 'tensor')
- new_key_momentum: float32 [8, 8192, 1024], P('gossip', 'fsdp', 'tensor')
- new_value_momentum: float32 [8, 8192, 1024], P('gossip', 'fsdp', 'tensor')
All inputs are finite; a program needn't handle non-finite values.
Results may differ from a plain program's by a relative error of at most 0.0055.
Values may be sent and summed in bfloat16 or wider, within the bound.
No kernel may reach another device: no remote copies, remote signals or barrier semaphores. Data moves between devices by JAX's collectives and lax.ppermute only.
A program may use at most 192 MiB of HBM per device.

v0:
```python
from functools import partial

import jax
import jax.numpy as jnp
from jax import lax
from jax.sharding import PartitionSpec as P

D = 8192


momentum_decay = 0.9
learn_rate = 0.5


def as_sent(shard):

    def short(part):
        return part.astype(jnp.bfloat16) if part.dtype == jnp.float32 else part

    return jax.tree.map(short, shard)


def swapped(shard, axis, distance):
    return lax.ppermute(shard, axis, [(i, i ^ 1 << distance) for i in range(lax.axis_size(axis))])


def swap_with(which, pair):
    return swapped((as_sent(pair[0]), as_sent(pair[1])), "gossip", which)


def per_device(
    normed,
    key_cotangent,
    value_cotangent,
    key_weight,
    value_weight,
    key_momentum,
    value_momentum,
    step_index,
):
    scaling = D ** (-0.5)
    local_cols = key_cotangent.shape[1]
    contract = (((0,), (0,)), ((), ()))
    transposed = (((1,), (1,)), ((), ()))
    key_half = key_weight[0].astype(jnp.bfloat16)
    value_half = value_weight[0].astype(jnp.bfloat16)
    cotangents = jnp.concatenate([key_cotangent, value_cotangent], axis=1)
    key_full, value_full = (
        lax.all_gather(key_half, "fsdp", axis=0, tiled=True),
        lax.all_gather(value_half, "fsdp", axis=0, tiled=True),
    )
    joined = jnp.concatenate([key_full, value_full], axis=1)
    gathered = lax.all_gather(normed, "tensor", axis=0, tiled=True)
    projected = jnp.dot(gathered, joined, preferred_element_type=jnp.float32) * scaling
    weight_terms = (
        lax.dot_general(gathered, cotangents, contract, preferred_element_type=jnp.float32)
        * scaling
    )
    input_grad = lax.psum_scatter(
        lax.dot_general(cotangents, joined, transposed, preferred_element_type=jnp.float32)
        * scaling,
        "tensor",
        scatter_dimension=0,
        tiled=True,
    ).astype(jnp.bfloat16)
    summed = lax.psum_scatter(
        weight_terms.astype(jnp.bfloat16), "fsdp", scatter_dimension=0, tiled=True
    ).astype(jnp.float32)
    projected_keys = projected[:, :local_cols].astype(jnp.bfloat16)
    projected_values = projected[:, local_cols:].astype(jnp.bfloat16)
    key_velocity = momentum_decay * key_momentum[0] + summed[:, :local_cols]
    value_velocity = momentum_decay * value_momentum[0] + summed[:, local_cols:]
    moved_key = key_weight[0] - learn_rate * key_velocity
    moved_value = value_weight[0] - learn_rate * value_velocity
    levels = lax.axis_size("gossip").bit_length() - 1
    branches = [partial(swap_with, which) for which in range(levels)]
    partner_key, partner_value = lax.switch(step_index % levels, branches, (moved_key, moved_value))
    new_key_weight = (0.5 * (moved_key + partner_key))[None]
    new_value_weight = (0.5 * (moved_value + partner_value))[None]
    return (
        projected_keys,
        projected_values,
        input_grad,
        new_key_weight,
        new_value_weight,
        key_velocity[None],
        value_velocity[None],
    )


def solution(mesh):
    in_specs = (
        P(("gossip", "fsdp", "tensor"), None),
        P(("gossip", "fsdp"), "tensor"),
        P(("gossip", "fsdp"), "tensor"),
        P("gossip", "fsdp", "tensor"),
        P("gossip", "fsdp", "tensor"),
        P("gossip", "fsdp", "tensor"),
        P("gossip", "fsdp", "tensor"),
        P(),
    )
    out_specs = (
        P(("gossip", "fsdp"), "tensor"),
        P(("gossip", "fsdp"), "tensor"),
        P(("gossip", "fsdp", "tensor"), None),
        P("gossip", "fsdp", "tensor"),
        P("gossip", "fsdp", "tensor"),
        P("gossip", "fsdp", "tensor"),
        P("gossip", "fsdp", "tensor"),
    )
    return jax.shard_map(
        per_device, mesh=mesh, in_specs=in_specs, out_specs=out_specs, check_vma=False
    )
```

profile of v0, /device:TPU:1, one launch (start us, length us, event | category | flops | bytes accessed | tf_op | source)
XLA Modules:
  0.0 303.8 jit_solution(5669386947220351665)
XLA Ops:
  7.9 1.9 copy.15
  15.2 47.9 %all-gather.8.cloned.1.call-done = bf16[512,8192]{1,0:T(8,128)(2,1)} async-done(((bf16[64,8192]{1,0:T(8,128)(2,1)}), bf16[512,8192]{1,0:T(8,128)(2,1)}) %all-gather.8.cloned.1.call-update) | async-done | bytes 8388624 | tf_op jit(solution)/shard_map/all_gather | solution.py:53
  63.1 7.8 %fusion.1 = bf16[8192,256]{0,1:T(8,128)(2,1)} fusion(bf16[512,256]{1,0:T(8,128)(2,1)S(1)} %constant_dynamic-update-slice_fusion.2, bf16[512,8192]{1,0:T(8,128)(2,1)} %all-gather.8.cloned.1.call-done), kind=kOutput, calls=%fused_computation.3 | convolution fusion | flops 2151677952 | bytes 12845056 | tf_op jit(solution)/shard_map/dot_general | solution.py:56
  71.0 29.9 %all-gather.4.cloned.1.call-done = bf16[8192,128]{0,1:T(8,128)(2,1)} async-done(((bf16[4096,128]{0,1:T(8,128)(2,1)}), bf16[8192,128]{0,1:T(8,128)(2,1)}) %all-gather.4.cloned.1.call-update) | async-done | bytes 2097168 | tf_op jit(solution)/shard_map/all_gather | solution.py:49
  100.8 3.1 %constant_dynamic-update-slice_fusion.1 = bf16[8192,256]{0,1:T(8,128)(2,1)} fusion(bf16[8192,128]{0,1:T(8,128)(2,1)} %all-gather.4.cloned.1.call-done), kind=kLoop, calls=%fused_computation.18 | loop fusion | bytes 4194304
  103.9 35.9 %all-gather.6.cloned.1.call-done = bf16[8192,128]{0,1:T(8,128)(2,1)} async-done(((bf16[4096,128]{0,1:T(8,128)(2,1)}), bf16[8192,128]{0,1:T(8,128)(2,1)}) %all-gather.6.cloned.1.call-update) | async-done | bytes 2097168 | tf_op jit(solution)/shard_map/all_gather | solution.py:50
  139.8 3.1 %constant_dynamic-update-slice_fusion = bf16[8192,256]{0,1:T(8,128)(2,1)} fusion(bf16[8192,256]{0,1:T(8,128)(2,1)} %constant_dynamic-update-slice_fusion.1, bf16[8192,128]{0,1:T(8,128)(2,1)} %all-gather.6.cloned.1.call-done), kind=kLoop, calls=%fused_computation.17 | loop fusion | bytes 4194304 | tf_op jit(solution)/shard_map/concatenate | solution.py:52
  142.9 10.8 %convolution_multiply_fusion = f32[512,8192]{1,0:T(8,128)} fusion(bf16[512,256]{1,0:T(8,128)(2,1)S(1)} %constant_dynamic-update-slice_fusion.2, bf16[8192,256]{0,1:T(8,128)(2,1)} %constant_dynamic-update-slice_fusion), kind=kOutput, calls=%fused_computation | convolution fusion | flops 2151677952 | bytes 21233664 | tf_op jit(solution)/shard_map/dot_general | solution.py:60
  157.1 2.9 copy.18
  160.0 7.2 %fusion.3 = bf16[512,256]{0,1:T(8,128)(2,1)S(1)} fusion(bf16[8192,256]{0,1:T(8,128)(2,1)} %constant_dynamic-update-slice_fusion, bf16[512,8192]{1,0:T(8,128)(2,1)} %all-gather.8.cloned.1.call-done), kind=kOutput, calls=%fused_computation.14 | convolution fusion | flops 2147745792 | bytes 12845056 | tf_op jit(solution)/shard_map/dot_general | solution.py:54
  168.8 31.2 %reduce-scatter.5.cloned.1.call-done = bf16[4096,256]{0,1:T(8,128)(2,1)} async-done(((bf16[8192,256]{0,1:T(8,128)(2,1)}), bf16[4096,256]{0,1:T(8,128)(2,1)}) %reduce-scatter.5.cloned.1.call-update) | async-done | bytes 2097168 | tf_op jit(solution)/shard_map/reduce_scatter | solution.py:66
  200.0 2.2 convert_element_type.65
  203.4 4.7 %fusion.5 = (f32[1,4096,128]{1,2,0:T(8,128)}, f32[4096,128]{0,1:T(8,128)S(1)}, f32[4096,128]{0,1:T(8,128)}, f32[1,4096,128]{1,2,0:T(8,128)}) fusion(f32[4096,256]{0,1:T(8,128)S(1)} %convert_element_type.65, f32[1,4096,128]{1,2,0:T(8,128)} %copy.18, f32[1,4096,128]{1,2,0:T(8,128)S(1)} %copy-done.3, f32[1,4096,128]{1,2,0:T(8,128)S(1)} %copy-done.4, ...), kind=kLoop, calls=%fused_computation.16 | loop fusion | flops 4194304 | bytes 20971520 | tf_op jit(solution)/shard_map/broadcast_in_dim | solution.py:87
  208.2 2.9 copy.32
  211.0 3.1 %copy.31 = f32[1,4096,128]{2,1,0:T(8,128)} copy(f32[1,4096,128]{1,2,0:T(8,128)} %get-tuple-element.63) | data formatting | bytes 4194304
  214.2 50.7 %conditional.3 = (f32[4096,128]{0,1:T(8,128)}, f32[4096,128]{0,1:T(8,128)}) conditional(s32[]{:T(128)} %clamp.3, (f32[4096,128]{0,1:T(8,128)}, f32[4096,128]{0,1:T(8,128)S(1)}) %tuple.40, (f32[4096,128]{0,1:T(8,128)}, f32[4096,128]{0,1:T(8,128)S(1)}) %tuple.40, (f32[4096,128]{0,1:T(8,128)}, f32[4096,128]{0,1:T(8,128)S(1)}) %tuple.40), branch_computations={%region_2.3_spmd, %region_3.4_spmd, %region_4.5_spmd} | conditional | bytes 20971616
  214.2 2.5 copy.21
  219.5 21.3 %collective-permute-done.2 = bf16[4096,128]{1,0:T(8,128)(2,1)} collective-permute-done((bf16[4096,128]{1,0:T(8,128)(2,1)}, bf16[4096,128]{1,0:T(8,128)(2,1)}, u32[]{:S(2)}, u32[]{:S(2)}) %collective-permute-start.2) | collective-permute-done | bytes 1048608 | tf_op jit(solution)/shard_map/cond/branch_1_fun/ppermute | solution.py:24
  240.8 2.6 copy.34
  243.4 19.9 %collective-permute-done.3 = bf16[4096,128]{1,0:T(8,128)(2,1)S(1)} collective-permute-done((bf16[4096,128]{1,0:T(8,128)(2,1)}, bf16[4096,128]{1,0:T(8,128)(2,1)S(1)}, u32[]{:S(2)}, u32[]{:S(2)}) %collective-permute-start.3) | collective-permute-done | bytes 1048608 | tf_op jit(solution)/shard_map/cond/branch_1_fun/ppermute | solution.py:24
  264.9 5.7 %multiply_bitcast_fusion = (f32[1,4096,128]{1,2,0:T(8,128)}, f32[1,4096,128]{1,2,0:T(8,128)}) fusion(f32[4096,128]{0,1:T(8,128)S(1)} %get-tuple-element.59, f32[4096,128]{0,1:T(8,128)} %get-tuple-element.57, f32[4096,128]{0,1:T(8,128)} %get-tuple-element.62, f32[4096,128]{0,1:T(8,128)} %get-tuple-element.56), kind=kLoop, calls=%fused_computation.10 | loop fusion | flops 2097152 | bytes 12582912 | tf_op jit(solution)/shard_map/broadcast_in_dim | solution.py:79
  270.6 3.0 %copy.30 = f32[1,4096,128]{2,1,0:T(8,128)} copy(f32[1,4096,128]{1,2,0:T(8,128)} %get-tuple-element.66) | data formatting | bytes 4194304
  275.4 19.2 %reduce-scatter.3.cloned.1.call-done = f32[64,8192]{1,0:T(8,128)} async-done(((f32[512,8192]{1,0:T(8,128)}), f32[64,8192]{1,0:T(8,128)}) %reduce-scatter.3.cloned.1.call-update) | async-done | bytes 2097168 | tf_op jit(solution)/shard_map/reduce_scatter | solution.py:59
  294.6 2.7 convert_element_type.62
  (42 shorter events, 17.7 us)
Async XLA Ops:
  7.2 56.0 %all-gather.8.cloned.1.call-start = ((), (), s32[]{:S(2)}) async-start(), calls=%async_computation.4 | async-start | bytes 9437184 | tf_op jit(solution)/shard_map/all_gather | solution.py:53
  7.9 92.9 %all-gather.4.cloned.1.call-start = ((), (), s32[]{:S(2)}) async-start(), calls=%async_computation.2 | async-start | bytes 3145728 | tf_op jit(solution)/shard_map/all_gather | solution.py:49
  9.9 1.7 copy-start
  11.5 128.2 %all-gather.6.cloned.1.call-start = ((), (), s32[]{:S(2)}) async-start(), calls=%async_computation.3 | async-start | bytes 3145728 | tf_op jit(solution)/shard_map/all_gather | solution.py:50
  13.5 1.7 copy-start.2
  13.5 1.7 copy-start.7
  13.5 1.7 copy-start.8
  15.1 184.8 %reduce-scatter.5.cloned.1.call-start = ((), (), s32[]{:S(2)}) async-start(), calls=%async_computation.6 | async-start | bytes 6291456 | tf_op jit(solution)/shard_map/reduce_scatter | solution.py:66
  70.9 223.7 %reduce-scatter.3.cloned.1.call-start = ((), (), s32[]{:S(2)}) async-start(), calls=%async_computation.5 | async-start | bytes 18874368 | tf_op jit(solution)/shard_map/reduce_scatter | solution.py:59
  153.7 1.6 copy-start.6
  199.9 2.2 copy-start.1
  199.9 2.9 copy-start.3
  200.0 3.5 %copy-start.4 = (f32[1,4096,128]{1,2,0:T(8,128)S(1)}, f32[1,4096,128]{1,2,0:T(8,128)}, u32[]{:S(2)}) copy-start(f32[1,4096,128]{1,2,0:T(8,128)} %copy.17) | copy-start | bytes 6291460
  216.7 24.1 %collective-permute-start.2 = (bf16[4096,128]{1,0:T(8,128)(2,1)}, bf16[4096,128]{1,0:T(8,128)(2,1)}, u32[]{:S(2)}, u32[]{:S(2)}) collective-permute-start(bf16[4096,128]{1,0:T(8,128)(2,1)} %copy.21), channel_id=1, source_target_pairs={{0,32},{16,48},{32,0},{48,16},{64,96},{80,112},{96,64},{112,80},{1... | collective-permute-start | bytes 3145736 | tf_op jit(solution)/shard_map/cond/branch_1_fun/ppermute | solution.py:24
  219.0 44.2 %collective-permute-start.3 = (bf16[4096,128]{1,0:T(8,128)(2,1)}, bf16[4096,128]{1,0:T(8,128)(2,1)S(1)}, u32[]{:S(2)}, u32[]{:S(2)}) collective-permute-start(bf16[4096,128]{1,0:T(8,128)(2,1)} %copy.22), channel_id=1, source_target_pairs={{0,32},{16,48},{32,0},{48,16},{64,96},{80,112},{96,64},{112,80},{1... | collective-permute-start | bytes 3145736 | tf_op jit(solution)/shard_map/cond/branch_1_fun/ppermute | solution.py:24
  270.6 3.0 %copy-start.5 = (f32[1,4096,128]{1,2,0:T(8,128)S(1)}, f32[1,4096,128]{1,2,0:T(8,128)}, u32[]{:S(2)}) copy-start(f32[1,4096,128]{1,2,0:T(8,128)} %get-tuple-element.67) | copy-start | bytes 6291460
Sparse Core Ops, SparseCore 0:
  9.7 53.3 all-gather.7
  65.3 35.4 all-gather.3
  103.1 36.6 all-gather.5
  142.0 57.8 reduce-scatter.4
  202.4 92.1 reduce-scatter.2
where the time goes:
time: 304 us
  waiting for transfers between devices  206 us (68%)
  local copies, waits for them, and re-layouts  38.2 us (13%)
  matrix products  25.8 us (8%)
  other arithmetic  17.6 us (6%)
  between operations  14.7 us (5%)
    all_gather x1, waiting for transfers between devices, per_device(): gathered = lax.all_gather(normed, 'tensor', axis=0, tiled=True)  47.9 us
    ppermute x2, waiting for transfers between devices, swapped(): lax.ppermute(shard, axis, [(i, i ^ 1 << distance) for i in range(lax.axis...  41.2 us
    all_gather x1, waiting for transfers between devices, per_device(): lax.all_gather(value_half, 'fsdp', axis=0, tiled=True)  35.9 us
    reduce_scatter x1, waiting for transfers between devices, per_device(): lax.psum_scatter(weight_terms.astype(jnp.bfloat16), 'fsdp', scatter_dimen...  31.2 us
    all_gather x1, waiting for transfers between devices, per_device(): lax.all_gather(key_half, 'fsdp', axis=0, tiled=True)  29.9 us
    unnamed x30, local copies, waits for them, and re-layouts  27 us
    reduce_scatter x1, waiting for transfers between devices, per_device(): lax.psum_scatter(lax.dot_general(cotangents, joined, transposed, preferre...  19.2 us
    dot_general x1, matrix products, per_device(): lax.dot_general(cotangents, joined, transposed, preferred_element_type=jn...  10.8 us
  transfers between devices with their start and end apart: 7, of which 7 were waited for; matrix products, arithmetic and copies ran while one was open for 25% of the time, Pallas kernels for 0%

commit v1 on v0

v1 whole, which is shorter than its diff:
```python
from functools import partial

import jax
import jax.numpy as jnp
from jax import lax
from jax.experimental import pallas as pl
from jax.experimental.pallas import tpu as pltpu
from jax.sharding import PartitionSpec as P

D = 8192
SCALING = D ** (-0.5)
momentum_decay = 0.9
learn_rate = 0.5

F32 = jnp.float32
BF = jnp.bfloat16
HALF = 4096
QUARTER = 2048
CHUNKS = 2
CH = QUARTER // CHUNKS
ROWS = 64
TOK = 512
COLS = 128
TILE = 512

MB = 1024 * 1024


def sds(shape, dtype):
    return jax.ShapeDtypeStruct(shape, dtype)


def params(mib):
    return pltpu.CompilerParams(vmem_limit_bytes=mib * MB)


def cost(flops, nbytes):
    return pl.CostEstimate(flops=flops, bytes_accessed=nbytes, transcendentals=0)


def smem():
    return pl.BlockSpec(memory_space=pltpu.SMEM)


def vmem():
    return pl.BlockSpec(memory_space=pltpu.VMEM)


def split_kernel(where, x, k, v, kv, *outs):
    f, c = where[0], where[2]
    kv[:, :COLS] = k[...]
    kv[:, COLS:] = v[...]
    quarters = (2 * f + c, 2 * f + 1 - c, 2 * (1 - f) + c, 2 * (1 - f) + 1 - c)
    at = 0
    for q in quarters:
        for h in range(CHUNKS):
            start = pl.multiple_of(q * QUARTER + h * CH, CH)
            outs[at][...] = x[:, pl.ds(start, CH)]
            at += 1


def split_inputs(where, x, k, v):
    piece = sds((ROWS, CH), BF)
    out = pl.pallas_call(
        split_kernel,
        out_shape=[sds((TOK, 2 * COLS), BF)] + [piece] * (4 * CHUNKS),
        in_specs=[smem(), vmem(), vmem(), vmem()],
        out_specs=[vmem()] * (1 + 4 * CHUNKS),
        compiler_params=params(8),
        cost_estimate=cost(0, 2_600_000),
        name="split_inputs",
    )(where, x, k, v)
    return out[0], [out[1 + CHUNKS * i : 1 + CHUNKS * (i + 1)] for i in range(4)]


def cast_kernel(where, ko, vo, kx, vx, own, other):
    own[:, :COLS] = ko[0].astype(BF)
    own[:, COLS:] = vo[0].astype(BF)
    other[:, :COLS] = kx[0].astype(BF)
    other[:, COLS:] = vx[0].astype(BF)


def cast_weights(where, kw, vw):
    n = QUARTER // TILE
    mine = pl.BlockSpec((1, TILE, COLS), lambda i, w: (0, w[2] * n + i, 0))
    theirs = pl.BlockSpec((1, TILE, COLS), lambda i, w: (0, (1 - w[2]) * n + i, 0))
    out = pl.BlockSpec((TILE, 2 * COLS), lambda i, w: (i, 0))
    shape = sds((QUARTER, 2 * COLS), BF)
    return pl.pallas_call(
        cast_kernel,
        out_shape=[shape, shape],
        grid_spec=pltpu.PrefetchScalarGridSpec(
            num_scalar_prefetch=1,
            grid=(n,),
            in_specs=[mine, mine, theirs, theirs],
            out_specs=[out, out],
        ),
        compiler_params=params(8),
        cost_estimate=cost(0, 6 * MB),
        name="cast_weights",
    )(where, kw, vw, kw, vw)


def order_kernel(where, own, core, other, othercore, out):
    y, c = where[1], where[2]
    for j in range(4):
        for cr in range(2):
            chip = lax.rem(y + j, 4)
            row = pl.multiple_of(chip * 2 * ROWS + (c + cr - 2 * c * cr) * ROWS, ROWS)
            to = j * 256 + cr * ROWS
            out[to : to + ROWS, : 2 * COLS] = own[pl.ds(row, ROWS), :]
            out[to : to + ROWS, 2 * COLS :] = core[pl.ds(row, ROWS), :]
            to += 128
            out[to : to + ROWS, : 2 * COLS] = other[pl.ds(row, ROWS), :]
            out[to : to + ROWS, 2 * COLS :] = othercore[pl.ds(row, ROWS), :]


def order_cotangents(where, own, core, other, othercore):
    return pl.pallas_call(
        order_kernel,
        out_shape=sds((1024, 512), BF),
        in_specs=[smem()] + [vmem()] * 4,
        out_specs=vmem(),
        compiler_params=params(8),
        cost_estimate=cost(0, 2 * MB),
        name="order_cotangents",
    )(where, own, core, other, othercore)


NT = (((1,), (1,)), ((), ()))
TN = (((0,), (0,)), ((), ()))
DXT = 512


def dx_kernel(kv, w0, w1, *outs):
    part = lax.dot_general(kv[:, :256], w0[...], NT, preferred_element_type=F32)
    part += lax.dot_general(kv[:, 256:], w1[...], NT, preferred_element_type=F32)
    part = (part * SCALING).astype(BF)
    for g in range(2):
        base = 128 * (1 - g)
        oa, ob, right, left, own = outs[5 * g : 5 * g + 5]
        oa[...] = part[512 + base : 512 + base + 64]
        ob[...] = part[512 + base + 64 : 512 + base + 128]
        right[...] = part[256 + base : 256 + base + 128]
        left[...] = part[768 + base : 768 + base + 128]
        own[...] = part[base : base + 128]


def input_terms(kv, w0, w1):
    small, large = sds((64, QUARTER), BF), sds((128, QUARTER), BF)
    sspec = pl.BlockSpec((64, DXT), lambda i: (0, i))
    lspec = pl.BlockSpec((128, DXT), lambda i: (0, i))
    wspec = pl.BlockSpec((DXT, 256), lambda i: (i, 0))
    return pl.pallas_call(
        dx_kernel,
        out_shape=[small, small, large, large, large] * 2,
        grid=(QUARTER // DXT,),
        in_specs=[pl.BlockSpec((1024, 512), lambda i: (0, 0)), wspec, wspec],
        out_specs=[sspec, sspec, lspec, lspec, lspec] * 2,
        compiler_params=params(16),
        cost_estimate=cost(2 * 1024 * 512 * QUARTER, 7 * MB),
        name="input_terms",
    )(kv, w0, w1)


def dw_kernel(kv, *refs):
    xs, (own, send) = refs[:8], refs[8:]
    x = jnp.concatenate([r[...] for r in xs], axis=0)
    g = lax.dot_general(x, kv[...], TN, preferred_element_type=F32) * SCALING
    own[...] = g[:, :256]
    send[...] = g[:, 256:].astype(BF)


def weight_terms(kv, xs):
    t = 256
    return pl.pallas_call(
        dw_kernel,
        out_shape=[sds((CH, 256), F32), sds((CH, 256), BF)],
        grid=(CH // t,),
        in_specs=[pl.BlockSpec((1024, 512), lambda i: (0, 0))]
        + [pl.BlockSpec((128, t), lambda i: (0, i))] * 8,
        out_specs=[pl.BlockSpec((t, 256), lambda i: (i, 0))] * 2,
        compiler_params=params(16),
        cost_estimate=cost(2 * 1024 * 512 * CH, 5 * MB),
        name="weight_terms",
    )(kv, *xs)


def proj_kernel(*refs):
    xs, (w0, w1), (own, send), acc = refs[:8], refs[8:10], refs[10:12], refs[12]
    i = pl.program_id(0)
    w = jnp.concatenate([w0[...], w1[...]], axis=1)
    x = jnp.concatenate([r[...] for r in xs], axis=0)
    part = jnp.dot(x, w, preferred_element_type=F32) * SCALING

    @pl.when(i == 0)
    def _():
        acc[...] = part

    @pl.when(i > 0)
    def _():
        acc[...] += part

    @pl.when(i == pl.num_programs(0) - 1)
    def _():
        own[...] = acc[:, :256]
        send[...] = acc[:, 256:].astype(BF)


def projection(chunk, prev, xs, w0, w1):
    t = 512
    n = CH // t
    wspec = pl.BlockSpec((t, 256), lambda i: (chunk * n + i, 0))
    return pl.pallas_call(
        proj_kernel,
        out_shape=[sds((1024, 256), F32), sds((1024, 256), BF)],
        grid=(n,),
        in_specs=[pl.BlockSpec((128, t), lambda i: (0, i))] * 8 + [wspec] * 2,
        out_specs=[pl.BlockSpec((1024, 256), lambda i: (0, 0))] * 2,
        scratch_shapes=[pltpu.VMEM((1024, 512), F32)],
        compiler_params=params(16),
        cost_estimate=cost(2 * 1024 * 512 * CH, 5 * MB),
        name="projection",
    )(*xs, w0, w1)


def proj_sum_kernel(a, b, ra, rb, keep, send):
    for at in range(0, 1024, 64):
        j, o, cr = at // 256, at // 128 % 2, at // 64 % 2
        far = at + 64 - 128 * cr
        total = (
            a[at : at + 64] + b[at : at + 64] + ra[far : far + 64].astype(F32) + rb[far : far + 64].astype(F32)
        )
        to = j * 128 + cr * 64
        if o:
            send[to : to + 64] = total.astype(BF)
        else:
            keep[to : to + 64] = total


def projection_sum(a, b, ra, rb):
    return pl.pallas_call(
        proj_sum_kernel,
        out_shape=[sds((512, 256), F32), sds((512, 256), BF)],
        in_specs=[vmem()] * 4,
        out_specs=[vmem()] * 2,
        compiler_params=params(8),
        cost_estimate=cost(0, 4 * MB),
        name="projection_sum",
    )(a, b, ra, rb)


def proj_end_kernel(where, keep, got, keys, values):
    y, c = where[1], where[2]
    for j in range(4):
        for cr in range(2):
            chip = lax.rem(y + j, 4)
            row = pl.multiple_of(chip * 2 * ROWS + (c + cr - 2 * c * cr) * ROWS, ROWS)
            at = j * 128 + cr * ROWS
            total = (keep[at : at + ROWS] + got[at : at + ROWS].astype(F32)).astype(BF)
            keys[pl.ds(row, ROWS), :] = total[:, :COLS]
            values[pl.ds(row, ROWS), :] = total[:, COLS:]


def projection_end(where, keep, got):
    out = sds((512, COLS), BF)
    return pl.pallas_call(
        proj_end_kernel,
        out_shape=[out, out],
        in_specs=[smem()] + [vmem()] * 2,
        out_specs=[vmem()] * 2,
        compiler_params=params(8),
        cost_estimate=cost(0, MB),
        name="projection_end",
    )(where, keep, got)


def sum3_kernel(a, b, c, lo, hi):
    total = (a[...].astype(F32) + b[...].astype(F32) + c[...].astype(F32)).astype(BF)
    lo[...] = total[:64]
    hi[...] = total[64:]


def sum3(a, b, c):
    out = sds((64, QUARTER), BF)
    return pl.pallas_call(
        sum3_kernel,
        out_shape=[out, out],
        in_specs=[vmem()] * 3,
        out_specs=[vmem()] * 2,
        compiler_params=params(8),
        cost_estimate=cost(0, 2 * MB),
        name="sum_terms",
    )(a, b, c)


def join_kernel(where, own, core, z, zc, out):
    f, c = where[0], where[2]
    quarters = (2 * f + c, 2 * f + 1 - c, 2 * (1 - f) + c, 2 * (1 - f) + 1 - c)
    for q, ref in zip(quarters, (own, core, z, zc)):
        out[:, pl.ds(pl.multiple_of(q * QUARTER, QUARTER), QUARTER)] = ref[...]


def join(where, own, core, z, zc):
    return pl.pallas_call(
        join_kernel,
        out_shape=sds((ROWS, D), BF),
        in_specs=[smem()] + [vmem()] * 4,
        out_specs=vmem(),
        compiler_params=params(8),
        cost_estimate=cost(0, 2 * MB),
        name="join_input_grad",
    )(where, own, core, z, zc)


def chunk_specs(chunk):
    n = CH // TILE
    per_quarter = QUARTER // TILE

    def at(s, i, w):
        q = s + w[2] - 2 * s * w[2]
        return (0, q * per_quarter + chunk * n + i, 0)

    whole = pl.BlockSpec((1, TILE, COLS), at)
    term = pl.BlockSpec((TILE, 256), lambda s, i, w: (i, 0))
    moved = pl.BlockSpec((TILE, 256), lambda s, i, w: (s * n + i, 0))
    return (2, n), whole, term, moved


def step_kernel(where, kw, vw, km, vm, own, got, *refs):
    nkm, nvm, moved = refs[-3:]
    s = pl.program_id(0)

    def run(g):
        k = momentum_decay * km[0] + g[:, :COLS]
        v = momentum_decay * vm[0] + g[:, COLS:]
        nkm[0] = k
        nvm[0] = v
        moved[:, :COLS] = (kw[0] - learn_rate * k).astype(BF)
        moved[:, COLS:] = (vw[0] - learn_rate * v).astype(BF)

    @pl.when(s == 0)
    def _():
        run(own[...])

    @pl.when(s == 1)
    def _():
        run(got[...].astype(F32))


def step(where, chunk, kw, vw, km, vm, own, got, before):
    grid, whole, term, moved = chunk_specs(chunk)
    full = sds((1, HALF, COLS), F32)
    extra = [] if before is None else list(before)
    anyspec = pl.BlockSpec(memory_space=pl.ANY)
    return pl.pallas_call(
        step_kernel,
        out_shape=[full, full, sds((2 * CH, 256), BF)],
        grid_spec=pltpu.PrefetchScalarGridSpec(
            num_scalar_prefetch=1,
            grid=grid,
            in_specs=[whole] * 4 + [term] * 2 + [anyspec] * len(extra),
            out_specs=[whole, whole, moved],
        ),
        input_output_aliases={7: 0, 8: 1} if extra else {},
        compiler_params=params(16),
        cost_estimate=cost(0, 8 * MB),
        name="momentum_step",
    )(where, kw, vw, km, vm, own, got, *extra)


def mean_kernel(where, kw, vw, nkm, nvm, got, *refs):
    nkw, nvw = refs[-2:]
    nkw[0] = 0.5 * ((kw[0] - learn_rate * nkm[0]) + got[:, :COLS].astype(F32))
    nvw[0] = 0.5 * ((vw[0] - learn_rate * nvm[0]) + got[:, COLS:].astype(F32))


def mean(where, chunk, kw, vw, nkm, nvm, got, before):
    grid, whole, term, moved = chunk_specs(chunk)
    full = sds((1, HALF, COLS), F32)
    extra = [] if before is None else list(before)
    anyspec = pl.BlockSpec(memory_space=pl.ANY)
    return pl.pallas_call(
        mean_kernel,
        out_shape=[full, full],
        grid_spec=pltpu.PrefetchScalarGridSpec(
            num_scalar_prefetch=1,
            grid=grid,
            in_specs=[whole] * 4 + [moved] + [anyspec] * len(extra),
            out_specs=[whole, whole],
        ),
        input_output_aliases={6: 0, 7: 1} if extra else {},
        compiler_params=params(16),
        cost_estimate=cost(0, 8 * MB),
        name="average",
    )(where, kw, vw, nkm, nvm, got, *extra)


def to_right(a):
    return lax.ppermute(a, "tensor", [(t, (t + 2) % 8) for t in range(8)])


def to_left(a):
    return lax.ppermute(a, "tensor", [(t, (t + 6) % 8) for t in range(8)])


def to_core(a):
    return lax.ppermute(a, "tensor", [(t, t ^ 1) for t in range(8)])


def to_z(a):
    return lax.ppermute(a, "fsdp", [(0, 1), (1, 0)])


def to_z_core(a):
    return lax.ppermute(a, ("fsdp", "tensor"), [(i, i ^ 9) for i in range(16)])


def to_partner(a, bit):
    n = lax.axis_size("gossip")
    return lax.ppermute(a, "gossip", [(i, i ^ (1 << bit)) for i in range(n)])


def whole_step(bit, where, normed, kc, vc, kw, vw, km, vm):
    kv_own, (x_own, x_core, x_z, x_zc) = split_inputs(where, normed, kc, vc)
    kv_z = to_z(kv_own)
    gathered = []
    for h in range(CHUNKS):
        a0 = jnp.concatenate([x_own[h], to_core(x_core[h])], axis=0)
        a3, a1 = to_right(a0), to_left(a0)
        b0 = jnp.concatenate([to_z(x_z[h]), to_z_core(x_zc[h])], axis=0)
        b3, b1 = to_right(b0), to_left(b0)
        a2, b2 = to_right(a3), to_left(b1)
        gathered.append([a0, b0, a1, b1, a2, b2, a3, b3])
    w_own, w_send = cast_weights(where, kw, vw)
    w_core = to_core(w_send)
    kv = order_cotangents(where, kv_own, to_core(kv_own), kv_z, to_core(kv_z))

    momenta, moved, weights = None, [], None
    for h in range(CHUNKS):
        own, send = weight_terms(kv, gathered[h])
        *momenta, m = step(where, h, kw, vw, km, vm, own, to_core(send), momenta)
        moved.append(m)
    got = [to_partner(m, bit) for m in moved]

    terms = input_terms(kv, w_own, w_core)
    ends = []
    for g in range(2):
        oa, ob, right, left, mine = terms[5 * g : 5 * g + 5]
        ra, rb = to_right(oa), to_left(ob)
        right = jnp.concatenate([right[:64] + ra, right[64:]], axis=0)
        left = jnp.concatenate([left[:64], left[64:] + rb], axis=0)
        ends.append(sum3(mine, to_right(right), to_left(left)))
    (o_z, o_zc), (s_own, s_core) = ends
    input_grad = join(where, s_own, to_core(s_core), to_z(o_z), to_z_core(o_zc))

    pa, sa = projection(0, None, gathered[0], w_own, w_core)
    pb, sb = projection(1, None, gathered[1], w_own, w_core)
    keep, send = projection_sum(pa, pb, to_core(sa), to_core(sb))
    keys, values = projection_end(where, keep, to_z(send))

    for h in range(CHUNKS):
        weights = mean(where, h, kw, vw, *momenta, got[h], weights)
    return keys, values, input_grad, *weights, *momenta


def per_device(normed, kc, vc, kw, vw, km, vm, step_index):
    t = lax.axis_index("tensor")
    where = jnp.stack([lax.axis_index("fsdp"), t // 2, t % 2]).astype(jnp.int32)
    levels = lax.axis_size("gossip").bit_length() - 1
    branches = [partial(whole_step, bit) for bit in range(levels)]
    return lax.switch(step_index % levels, branches, where, normed, kc, vc, kw, vw, km, vm)


def solution(mesh):
    rows = P(("gossip", "fsdp", "tensor"), None)
    heads = P(("gossip", "fsdp"), "tensor")
    weight = P("gossip", "fsdp", "tensor")
    return jax.shard_map(
        per_device,
        mesh=mesh,
        in_specs=(rows, heads, heads, weight, weight, weight, weight, P()),
        out_specs=(heads, heads, rows, weight, weight, weight, weight),
        check_vma=False,
    )
```

time: 304 us -> 174 us (0.57)
  waiting for transfers between devices: 206 us -> 60.4 us
  starting transfers between devices: 1.59 us -> 66.7 us
  local copies, waits for them, and re-layouts: 38.2 us -> 1.12 us
  Pallas kernels: 0 us -> 33.6 us
  matrix products: 25.8 us -> 0 us
  other arithmetic: 17.6 us -> 0.42 us
  between operations: 14.7 us -> 1.57 us
  loops' own time: 0.01 us -> 7.51 us
    all_gather x3 -> x0, waiting for transfers between devices: 114 us -> none  [the longest x1 47.9 us: per_device(): gathered = lax.all_gather(normed, 'tensor', axis=0, tiled=True)]
    ppermute x2 -> x40, starting transfers between devices: 1.47 us -> 66.7 us  [the longest x10 29.5 us: to_left(): return lax.ppermute(a, 'tensor', [(t, (t + 6) % 8) for t in range(8)])]
    reduce_scatter x2 -> x0, waiting for transfers between devices: 50.4 us -> none  [the longest x1 31.2 us: per_device(): lax.psum_scatter(weight_terms.astype(jnp.bfloat16), 'fsdp', scatter_dimen...]
    pallas_call x0 -> x17, Pallas kernels: none -> 33.6 us  [the longest x2 8.72 us: mean(): pl.pallas_call(mean_kernel, out_shape=[full, full], grid_spec=pltpu.Prefe...]
    unnamed x30 -> x6, local copies, waits for them, and re-layouts: 27 us -> 1.02 us
    dot_general x3 -> x0, matrix products: 25.8 us -> none  [the longest x1 10.8 us: per_device(): lax.dot_general(cotangents, joined, transposed, preferred_element_type=jn...]
    ppermute x2 -> x40, waiting for transfers between devices: 41.2 us -> 60.4 us  [the longest x10 22.2 us: to_left(): return lax.ppermute(a, 'tensor', [(t, (t + 6) % 8) for t in range(8)])]
    broadcast_in_dim x2 -> x0, other arithmetic: 10.4 us -> none  [the longest x1 5.67 us: per_device(): new_value_weight = (0.5 * (moved_value + partner_value))[None]]
  transfers between devices with their start and end apart: 7 -> 40, of which waited for: 7 -> 16; matrix products, arithmetic and copies ran while one was open for 25% -> 0% of each run, Pallas kernels for 0% -> 16%
where the time goes in v1:
time: 174 us; the launch traced here: 171 us
  starting transfers between devices  66.7 us (38%)
  waiting for transfers between devices  60.4 us (35%)
  Pallas kernels  33.6 us (19%)
  loops' own time  7.51 us (4%)
    ppermute x10, starting transfers between devices, to_left(): return lax.ppermute(a, 'tensor', [(t, (t + 6) % 8) for t in range(8)])  29.5 us
    ppermute x10, waiting for transfers between devices, to_left(): return lax.ppermute(a, 'tensor', [(t, (t + 6) % 8) for t in range(8)])  22.2 us
    ppermute x5, waiting for transfers between devices, to_z(): return lax.ppermute(a, 'fsdp', [(0, 1), (1, 0)])  19.6 us
    ppermute x10, starting transfers between devices, to_core(): return lax.ppermute(a, 'tensor', [(t, t ^ 1) for t in range(8)])  15 us
    ppermute x3, waiting for transfers between devices, to_z_core(): return lax.ppermute(a, ('fsdp', 'tensor'), [(i, i ^ 9) for i in range(16)])  12.4 us
    pallas_call x2, Pallas kernels, mean(): pl.pallas_call(mean_kernel, out_shape=[full, full], grid_spec=pltpu.Prefe...  8.72 us
    ppermute x3, starting transfers between devices, to_z_core(): return lax.ppermute(a, ('fsdp', 'tensor'), [(i, i ^ 9) for i in range(16)])  7.64 us
    another operation x1, loops' own time, per_device(): lax.switch(step_index % levels, branches, where, normed, kc, vc, kw, vw,...  7.51 us
  transfers between devices with their start and end apart: 40, of which 16 were waited for; matrix products, arithmetic and copies ran while one was open for 0% of the time, Pallas kernels for 16%

profile of v1, /device:TPU:1, one launch (start us, length us, event | category | flops | bytes accessed | tf_op | source)
XLA Modules:
  0.0 171.3 jit_solution(11772436855240242881)
XLA Ops:
  1.4 168.6 %conditional.1 = (bf16[512,128]{1,0:T(8,128)(2,1)S(1)}, bf16[512,128]{1,0:T(8,128)(2,1)S(1)}, f32[1,4096,128]{2,1,0:T(8,128)}, f32[1,4096,128]{2,1,0:T(8,128)}, ...) conditional(s32[]{:T(128)} %clamp.3, (s32[3]{0:T(128)S(1)}, ...), branch_computations={%region_0.1_spmd, %region_1.2_spmd, %region_2.3_spmd} | conditional | flops 6447169536 | bytes 186102496 | solution.py:472
  7.8 3.5 %cast_weights.3 = (bf16[2048,256]{1,0:T(8,128)(2,1)S(1)}, bf16[2048,256]{1,0:T(8,128)(2,1)S(1)}) custom-call(s32[3]{0:T(128)S(1)} %get-tuple-element.48.where, f32[1,4096,128]{2,1,0:T(8,128)} %get-tuple-element.251.ko.kx.kw, f32[1,4096,128]{2,1,0:T(8,128)} %get-tuple-element.254.vo.vx.vw, f32[1,4096,128]{2,1,0:T(8,128)} %get-tuple-element.251.ko.kx.kw, ...), custom_call_target="tpu_custom_call" | custom-call | bytes 6291456 | tf_op jit(solution)/shard_map/cond/branch_0_fun/cast_weights/pallas_call | solution.py:89
  11.4 2.8 %collective-permute-done.1 = bf16[64,1024]{1,0:T(8,128)(2,1)S(1)} collective-permute-done((bf16[64,1024]{1,0:T(8,128)(2,1)S(1)}, bf16[64,1024]{1,0:T(8,128)(2,1)S(1)}, u32[]{:S(2)}, u32[]{:S(2)}) %collective-permute-start.1) | collective-permute-done | bytes 131104 | tf_op jit(solution)/shard_map/cond/branch_0_fun/ppermute | solution.py:412
  21.1 5.3 %collective-permute-done.12 = bf16[64,1024]{1,0:T(8,128)(2,1)S(1)} collective-permute-done((bf16[64,1024]{1,0:T(8,128)(2,1)S(1)}, bf16[64,1024]{1,0:T(8,128)(2,1)S(1)}, u32[]{:S(2)}, u32[]{:S(2)}) %collective-permute-start.12) | collective-permute-done | bytes 131104 | tf_op jit(solution)/shard_map/cond/branch_0_fun/ppermute | solution.py:416
  26.6 2.8 %collective-permute-start.14 = (bf16[128,1024]{1,0:T(8,128)(2,1)S(1)}, bf16[128,1024]{1,0:T(8,128)(2,1)S(1)}, u32[]{:S(2)}, u32[]{:S(2)}) collective-permute-start(bf16[128,1024]{1,0:T(8,128)(2,1)S(1)} %constant_dynamic-update-slice_fusion.6.refs_1_), channel_id=1, source_target_pairs={{0,6},{1,7},{2,0},{3,1},{4,2},{5,3},{6,4},{7,5},{8,14},{9,15},{10,... | collective-permute-start | bytes 786440 | tf_op jit(solution)/shard_map/cond/branch_0_fun/ppermute | solution.py:404
  29.5 2.7 %collective-permute-start.4 = (bf16[128,1024]{1,0:T(8,128)(2,1)S(1)}, bf16[128,1024]{1,0:T(8,128)(2,1)S(1)}, u32[]{:S(2)}, u32[]{:S(2)}) collective-permute-start(bf16[128,1024]{1,0:T(8,128)(2,1)S(1)} %constant_dynamic-update-slice_fusion.2.refs_1_), channel_id=1, source_target_pairs={{0,6},{1,7},{2,0},{3,1},{4,2},{5,3},{6,4},{7,5},{8,14},{9,15},{10,... | collective-permute-start | bytes 786440 | tf_op jit(solution)/shard_map/cond/branch_0_fun/ppermute | solution.py:404
  34.7 3.4 %collective-permute-start.3 = (bf16[128,1024]{1,0:T(8,128)(2,1)S(1)}, bf16[128,1024]{1,0:T(8,128)(2,1)S(1)}, u32[]{:S(2)}, u32[]{:S(2)}) collective-permute-start(bf16[128,1024]{1,0:T(8,128)(2,1)S(1)} %constant_dynamic-update-slice_fusion.refs_0_), channel_id=1, source_target_pairs={{0,6},{1,7},{2,0},{3,1},{4,2},{5,3},{6,4},{7,5},{8,14},{9,15},{10,... | collective-permute-start | bytes 786440 | tf_op jit(solution)/shard_map/cond/branch_0_fun/ppermute | solution.py:404
  40.6 3.1 %collective-permute-start.7 = (bf16[128,1024]{1,0:T(8,128)(2,1)S(1)}, bf16[128,1024]{1,0:T(8,128)(2,1)S(1)}, u32[]{:S(2)}, u32[]{:S(2)}) collective-permute-start(bf16[128,1024]{1,0:T(8,128)(2,1)S(1)} %collective-permute-done.4.refs_3_), channel_id=1, source_target_pairs={{0,6},{1,7},{2,0},{3,1},{4,2},{5,3},{6,4},{7,5},{8,14},{9,15},{10,... | collective-permute-start | bytes 786440 | tf_op jit(solution)/shard_map/cond/branch_0_fun/ppermute | solution.py:404
  45.9 3.4 %collective-permute-start.13 = (bf16[128,1024]{1,0:T(8,128)(2,1)S(1)}, bf16[128,1024]{1,0:T(8,128)(2,1)S(1)}, u32[]{:S(2)}, u32[]{:S(2)}) collective-permute-start(bf16[128,1024]{1,0:T(8,128)(2,1)S(1)} %constant_dynamic-update-slice_fusion.4.refs_0_), channel_id=1, source_target_pairs={{0,6},{1,7},{2,0},{3,1},{4,2},{5,3},{6,4},{7,5},{8,14},{9,15},{10,... | collective-permute-start | bytes 786440 | tf_op jit(solution)/shard_map/cond/branch_0_fun/ppermute | solution.py:404
  67.2 3.3 %input_terms.3 = (bf16[64,2048]{1,0:T(8,128)(2,1)S(1)}, bf16[64,2048]{1,0:T(8,128)(2,1)S(1)}, bf16[128,2048]{1,0:T(8,128)(2,1)S(1)}, bf16[128,2048]{1,0:T(8,128)...) custom-call(bf16[1024,512]{1,0:T(8,128)(2,1)S(1)} %order_cotangents., ...), custom_call_target="tpu_custom_call" | custom-call | flops 2147483648 | bytes 7340032 | tf_op jit(solution)/shard_map/cond/branch_0_fun/input_terms/pallas_call | solution.py:154
  83.9 2.7 %collective-permute-start.32 = (bf16[64,2048]{1,0:T(8,128)(2,1)S(1)}, bf16[64,2048]{1,0:T(8,128)(2,1)S(1)}, u32[]{:S(2)}, u32[]{:S(2)}) collective-permute-start(bf16[64,2048]{1,0:T(8,128)(2,1)S(1)} %get-tuple-element.84), channel_id=1, source_target_pairs={{0,6},{1,7},{2,0},{3,1},{4,2},{5,3},{6,4},{7,5},{8,14},{9,15},{10,... | collective-permute-start | bytes 786440 | tf_op jit(solution)/shard_map/cond/branch_0_fun/ppermute | solution.py:404
  86.7 3.7 %collective-permute-start.38 = (bf16[2048,256]{1,0:T(8,128)(2,1)S(1)}, bf16[2048,256]{1,0:T(8,128)(2,1)S(1)}, u32[]{:S(2)}, u32[]{:S(2)}) collective-permute-start(bf16[2048,256]{1,0:T(8,128)(2,1)S(1)} %get-tuple-element.97), channel_id=1, source_target_pairs={{0,16},{16,0},{32,48},{48,32},{64,80},{80,64},{96,112},{112,96},{1... | collective-permute-start | bytes 3145736 | tf_op jit(solution)/shard_map/cond/branch_0_fun/ppermute | solution.py:421
  91.3 3.7 %collective-permute-start.39 = (bf16[2048,256]{1,0:T(8,128)(2,1)S(1)}, bf16[2048,256]{1,0:T(8,128)(2,1)S(1)}, u32[]{:S(2)}, u32[]{:S(2)}) collective-permute-start(bf16[2048,256]{1,0:T(8,128)(2,1)S(1)} %get-tuple-element.98), channel_id=1, source_target_pairs={{0,16},{16,0},{32,48},{48,32},{64,80},{80,64},{96,112},{112,96},{1... | collective-permute-start | bytes 3145736 | tf_op jit(solution)/shard_map/cond/branch_0_fun/ppermute | solution.py:421
  95.1 3.5 %collective-permute-start.33 = (bf16[128,2048]{1,0:T(8,128)(2,1)S(1)}, bf16[128,2048]{1,0:T(8,128)(2,1)S(1)}, u32[]{:S(2)}, u32[]{:S(2)}) collective-permute-start(bf16[128,2048]{1,0:T(8,128)(2,1)S(1)} %pad_maximum_fusion.3), channel_id=1, source_target_pairs={{0,6},{1,7},{2,0},{3,1},{4,2},{5,3},{6,4},{7,5},{8,14},{9,15},{10,... | collective-permute-start | bytes 1572872 | tf_op jit(solution)/shard_map/cond/branch_0_fun/ppermute | solution.py:404
  98.8 2.7 %collective-permute-start.28 = (bf16[128,2048]{1,0:T(8,128)(2,1)S(1)}, bf16[128,2048]{1,0:T(8,128)(2,1)S(1)}, u32[]{:S(2)}, u32[]{:S(2)}) collective-permute-start(bf16[128,2048]{1,0:T(8,128)(2,1)S(1)} %pad_maximum_fusion.1), channel_id=1, source_target_pairs={{0,6},{1,7},{2,0},{3,1},{4,2},{5,3},{6,4},{7,5},{8,14},{9,15},{10,... | collective-permute-start | bytes 1572872 | tf_op jit(solution)/shard_map/cond/branch_0_fun/ppermute | solution.py:404
  101.6 6.1 %collective-permute-done.33.c = bf16[128,2048]{1,0:T(8,128)(2,1)S(1)} collective-permute-done((bf16[128,2048]{1,0:T(8,128)(2,1)S(1)}, bf16[128,2048]{1,0:T(8,128)(2,1)S(1)}, u32[]{:S(2)}, u32[]{:S(2)}) %collective-permute-start.33) | collective-permute-done | bytes 524320 | tf_op jit(solution)/shard_map/cond/branch_0_fun/ppermute | solution.py:404
  107.9 3.1 %collective-permute-done.31.b = bf16[128,2048]{1,0:T(8,128)(2,1)S(1)} collective-permute-done((bf16[128,2048]{1,0:T(8,128)(2,1)S(1)}, bf16[128,2048]{1,0:T(8,128)(2,1)S(1)}, u32[]{:S(2)}, u32[]{:S(2)}) %collective-permute-start.31) | collective-permute-done | bytes 524320 | tf_op jit(solution)/shard_map/cond/branch_0_fun/ppermute | solution.py:400
  111.6 7.4 %collective-permute-done.28.c = bf16[128,2048]{1,0:T(8,128)(2,1)S(1)} collective-permute-done((bf16[128,2048]{1,0:T(8,128)(2,1)S(1)}, bf16[128,2048]{1,0:T(8,128)(2,1)S(1)}, u32[]{:S(2)}, u32[]{:S(2)}) %collective-permute-start.28) | collective-permute-done | bytes 524320 | tf_op jit(solution)/shard_map/cond/branch_0_fun/ppermute | solution.py:404
  120.8 5.0 %collective-permute-start.35 = (bf16[64,2048]{1,0:T(8,128)(2,1)S(1)}, bf16[64,2048]{1,0:T(8,128)(2,1)S(1)}, u32[]{:S(2)}, u32[]{:S(2)}) collective-permute-start(bf16[64,2048]{1,0:T(8,128)(2,1)S(1)} %get-tuple-element.86), channel_id=1, source_target_pairs={{0,9},{1,8},{2,11},{3,10},{4,13},{5,12},{6,15},{7,14},{8,1},{9,0},... | collective-permute-start | bytes 786440 | tf_op jit(solution)/shard_map/cond/branch_0_fun/ppermute | solution.py:416
  126.0 14.9 %collective-permute-done.21.got = bf16[512,256]{1,0:T(8,128)(2,1)S(1)} collective-permute-done((bf16[512,256]{1,0:T(8,128)(2,1)S(1)}, bf16[512,256]{1,0:T(8,128)(2,1)S(1)}, u32[]{:S(2)}, u32[]{:S(2)}) %collective-permute-start.21) | collective-permute-done | bytes 262176 | tf_op jit(solution)/shard_map/cond/branch_0_fun/ppermute | solution.py:412
  140.9 3.8 %collective-permute-start.29 = (bf16[64,2048]{1,0:T(8,128)(2,1)S(1)}, bf16[64,2048]{1,0:T(8,128)(2,1)S(1)}, u32[]{:S(2)}, u32[]{:S(2)}) collective-permute-start(bf16[64,2048]{1,0:T(8,128)(2,1)S(1)} %get-tuple-element.79), channel_id=1, source_target_pairs={{0,1},{1,0},{2,3},{3,2},{4,5},{5,4},{6,7},{7,6},{8,9},{9,8},{10,11... | collective-permute-start | bytes 786440 | tf_op jit(solution)/shard_map/cond/branch_0_fun/ppermute | solution.py:408
  146.5 7.0 %collective-permute-done.35.zc = bf16[64,2048]{1,0:T(8,128)(2,1)S(1)} collective-permute-done((bf16[64,2048]{1,0:T(8,128)(2,1)S(1)}, bf16[64,2048]{1,0:T(8,128)(2,1)S(1)}, u32[]{:S(2)}, u32[]{:S(2)}) %collective-permute-start.35) | collective-permute-done | bytes 262176 | tf_op jit(solution)/shard_map/cond/branch_0_fun/ppermute | solution.py:416
  154.1 4.4 %average.6 = (f32[1,4096,128]{2,1,0:T(8,128)}, f32[1,4096,128]{2,1,0:T(8,128)}) custom-call(s32[3]{0:T(128)S(1)} %get-tuple-element.48.where, f32[1,4096,128]{2,1,0:T(8,128)S(1)} %copy-done, f32[1,4096,128]{2,1,0:T(8,128)S(1)} %copy-done.3, f32[1,4096,128]{2,1,0:T(8,128)} %get-tuple-element.291.nkm, f32[1,4096,128]{2,1,0:T(8,128)} %get-tuple-element.292.nvm, ...), custom_call_target="tpu_custom_call" | custom-call | bytes 8388608 | tf_op jit(solution)/shard_map/cond/branch_0_fun/average/pallas_call | solution.py:383
  158.5 4.4 %average.7 = (f32[1,4096,128]{2,1,0:T(8,128)}, f32[1,4096,128]{2,1,0:T(8,128)}) custom-call(s32[3]{0:T(128)S(1)} %get-tuple-element.48.where, f32[1,4096,128]{2,1,0:T(8,128)S(1)} %copy-done, f32[1,4096,128]{2,1,0:T(8,128)S(1)} %copy-done.3, f32[1,4096,128]{2,1,0:T(8,128)} %get-tuple-element.291.nkm, ...), custom_call_target="tpu_custom_call", output_to_operand_aliasing={{0}: (6, {}), {1}: (7, {})} | custom-call | bytes 8388608 | tf_op jit(solution)/shard_map/cond/branch_0_fun/average/pallas_call | solution.py:383
  (105 shorter events, 59.6 us)
Async XLA Ops:
  2.8 26.6 %collective-permute-start.23 = (bf16[512,256]{1,0:T(8,128)(2,1)S(1)}, bf16[512,256]{1,0:T(8,128)(2,1)S(1)}, u32[]{:S(2)}, u32[]{:S(2)}) collective-permute-start(bf16[512,256]{1,0:T(8,128)(2,1)S(1)} %get-tuple-element.72.own), channel_id=1, source_target_pairs={{0,8},{8,0},{1,9},{9,1},{2,10},{10,2},{3,11},{11,3},{4,12},{12,4},... | collective-permute-start | bytes 786440 | tf_op jit(solution)/shard_map/cond/branch_0_fun/ppermute | solution.py:412
  5.4 24.1 %collective-permute-start.22 = (bf16[512,256]{1,0:T(8,128)(2,1)S(1)}, bf16[512,256]{1,0:T(8,128)(2,1)S(1)}, u32[]{:S(2)}, u32[]{:S(2)}) collective-permute-start(bf16[512,256]{1,0:T(8,128)(2,1)S(1)} %get-tuple-element.72.own), channel_id=1, source_target_pairs={{0,1},{1,0},{2,3},{3,2},{4,5},{5,4},{6,7},{7,6},{8,9},{9,8},{10,11... | collective-permute-start | bytes 786440 | tf_op jit(solution)/shard_map/cond/branch_0_fun/ppermute | solution.py:408
  6.3 13.4 %collective-permute-start = (bf16[64,1024]{1,0:T(8,128)(2,1)S(1)}, bf16[64,1024]{1,0:T(8,128)(2,1)S(1)}, u32[]{:S(2)}, u32[]{:S(2)}) collective-permute-start(bf16[64,1024]{1,0:T(8,128)(2,1)S(1)} %get-tuple-element.53), channel_id=1, source_target_pairs={{0,1},{1,0},{2,3},{3,2},{4,5},{5,4},{6,7},{7,6},{8,9},{9,8},{10,11... | collective-permute-start | bytes 393224 | tf_op jit(solution)/shard_map/cond/branch_0_fun/ppermute | solution.py:408
  19.8 12.4 %collective-permute-start.15 = (bf16[128,1024]{1,0:T(8,128)(2,1)S(1)}, bf16[128,1024]{1,0:T(8,128)(2,1)S(1)}, u32[]{:S(2)}, u32[]{:S(2)}) collective-permute-start(bf16[128,1024]{1,0:T(8,128)(2,1)S(1)} %constant_dynamic-update-slice_fusion.4.refs_0_), channel_id=1, source_target_pairs={{0,2},{1,3},{2,4},{3,5},{4,6},{5,7},{6,0},{7,1},{8,10},{9,11},{10,... | collective-permute-start | bytes 786440 | tf_op jit(solution)/shard_map/cond/branch_0_fun/ppermute | solution.py:400
  26.5 40.8 %collective-permute-start.9 = (bf16[2048,256]{1,0:T(8,128)(2,1)S(1)}, bf16[2048,256]{1,0:T(8,128)(2,1)S(1)}, u32[]{:S(2)}, u32[]{:S(2)}) collective-permute-start(bf16[2048,256]{1,0:T(8,128)(2,1)S(1)} %get-tuple-element.59), channel_id=1, source_target_pairs={{0,1},{1,0},{2,3},{3,2},{4,5},{5,4},{6,7},{7,6},{8,9},{9,8},{10,11... | collective-permute-start | bytes 3145736 | tf_op jit(solution)/shard_map/cond/branch_0_fun/ppermute | solution.py:408
  32.2 11.5 %collective-permute-start.5 = (bf16[128,1024]{1,0:T(8,128)(2,1)S(1)}, bf16[128,1024]{1,0:T(8,128)(2,1)S(1)}, u32[]{:S(2)}, u32[]{:S(2)}) collective-permute-start(bf16[128,1024]{1,0:T(8,128)(2,1)S(1)} %constant_dynamic-update-slice_fusion.refs_0_), channel_id=1, source_target_pairs={{0,2},{1,3},{2,4},{3,5},{4,6},{5,7},{6,0},{7,1},{8,10},{9,11},{10,... | collective-permute-start | bytes 786440 | tf_op jit(solution)/shard_map/cond/branch_0_fun/ppermute | solution.py:400
  34.7 11.2 %collective-permute-start.3 = (bf16[128,1024]{1,0:T(8,128)(2,1)S(1)}, bf16[128,1024]{1,0:T(8,128)(2,1)S(1)}, u32[]{:S(2)}, u32[]{:S(2)}) collective-permute-start(bf16[128,1024]{1,0:T(8,128)(2,1)S(1)} %constant_dynamic-update-slice_fusion.refs_0_), channel_id=1, source_target_pairs={{0,6},{1,7},{2,0},{3,1},{4,2},{5,3},{6,4},{7,5},{8,14},{9,15},{10,... | collective-permute-start | bytes 786440 | tf_op jit(solution)/shard_map/cond/branch_0_fun/ppermute | solution.py:404
  45.9 11.9 %collective-permute-start.13 = (bf16[128,1024]{1,0:T(8,128)(2,1)S(1)}, bf16[128,1024]{1,0:T(8,128)(2,1)S(1)}, u32[]{:S(2)}, u32[]{:S(2)}) collective-permute-start(bf16[128,1024]{1,0:T(8,128)(2,1)S(1)} %constant_dynamic-update-slice_fusion.4.refs_0_), channel_id=1, source_target_pairs={{0,6},{1,7},{2,0},{3,1},{4,2},{5,3},{6,4},{7,5},{8,14},{9,15},{10,... | collective-permute-start | bytes 786440 | tf_op jit(solution)/shard_map/cond/branch_0_fun/ppermute | solution.py:404
  57.8 18.2 %collective-permute-start.37 = (bf16[1024,256]{1,0:T(8,128)(2,1)S(1)}, bf16[1024,256]{1,0:T(8,128)(2,1)S(1)}, u32[]{:S(2)}, u32[]{:S(2)}) collective-permute-start(bf16[1024,256]{1,0:T(8,128)(2,1)S(1)} %get-tuple-element.92), channel_id=1, source_target_pairs={{0,1},{1,0},{2,3},{3,2},{4,5},{5,4},{6,7},{7,6},{8,9},{9,8},{10,11... | collective-permute-start | bytes 1572872 | tf_op jit(solution)/shard_map/cond/branch_0_fun/ppermute | solution.py:408
  65.0 16.3 %collective-permute-start.36 = (bf16[1024,256]{1,0:T(8,128)(2,1)S(1)}, bf16[1024,256]{1,0:T(8,128)(2,1)S(1)}, u32[]{:S(2)}, u32[]{:S(2)}) collective-permute-start(bf16[1024,256]{1,0:T(8,128)(2,1)S(1)} %get-tuple-element.90), channel_id=1, source_target_pairs={{0,1},{1,0},{2,3},{3,2},{4,5},{5,4},{6,7},{7,6},{8,9},{9,8},{10,11... | collective-permute-start | bytes 1572872 | tf_op jit(solution)/shard_map/cond/branch_0_fun/ppermute | solution.py:408
  70.6 13.4 %collective-permute-start.25 = (bf16[64,2048]{1,0:T(8,128)(2,1)S(1)}, bf16[64,2048]{1,0:T(8,128)(2,1)S(1)}, u32[]{:S(2)}, u32[]{:S(2)}) collective-permute-start(bf16[64,2048]{1,0:T(8,128)(2,1)S(1)} %get-tuple-element.75), channel_id=1, source_target_pairs={{0,2},{1,3},{2,4},{3,5},{4,6},{5,7},{6,0},{7,1},{8,10},{9,11},{10,... | collective-permute-start | bytes 786440 | tf_op jit(solution)/shard_map/cond/branch_0_fun/ppermute | solution.py:400
  72.9 25.7 %collective-permute-start.20 = (bf16[1024,256]{1,0:T(8,128)(2,1)S(1)}, bf16[1024,256]{1,0:T(8,128)(2,1)S(1)}, u32[]{:S(2)}, u32[]{:S(2)}) collective-permute-start(bf16[1024,256]{1,0:T(8,128)(2,1)S(1)} %get-tuple-element.67), channel_id=1, source_target_pairs={{0,1},{1,0},{2,3},{3,2},{4,5},{5,4},{6,7},{7,6},{8,9},{9,8},{10,11... | collective-permute-start | bytes 1572872 | tf_op jit(solution)/shard_map/cond/branch_0_fun/ppermute | solution.py:408
  75.6 23.2 %collective-permute-start.19 = (bf16[1024,256]{1,0:T(8,128)(2,1)S(1)}, bf16[1024,256]{1,0:T(8,128)(2,1)S(1)}, u32[]{:S(2)}, u32[]{:S(2)}) collective-permute-start(bf16[1024,256]{1,0:T(8,128)(2,1)S(1)} %get-tuple-element.66), channel_id=1, source_target_pairs={{0,1},{1,0},{2,3},{3,2},{4,5},{5,4},{6,7},{7,6},{8,9},{9,8},{10,11... | collective-permute-start | bytes 1572872 | tf_op jit(solution)/shard_map/cond/branch_0_fun/ppermute | solution.py:408
  81.3 13.8 %collective-permute-start.30 = (bf16[64,2048]{1,0:T(8,128)(2,1)S(1)}, bf16[64,2048]{1,0:T(8,128)(2,1)S(1)}, u32[]{:S(2)}, u32[]{:S(2)}) collective-permute-start(bf16[64,2048]{1,0:T(8,128)(2,1)S(1)} %get-tuple-element.82), channel_id=1, source_target_pairs={{0,2},{1,3},{2,4},{3,5},{4,6},{5,7},{6,0},{7,1},{8,10},{9,11},{10,... | collective-permute-start | bytes 786440 | tf_op jit(solution)/shard_map/cond/branch_0_fun/ppermute | solution.py:400
  86.7 71.9 %collective-permute-start.38 = (bf16[2048,256]{1,0:T(8,128)(2,1)S(1)}, bf16[2048,256]{1,0:T(8,128)(2,1)S(1)}, u32[]{:S(2)}, u32[]{:S(2)}) collective-permute-start(bf16[2048,256]{1,0:T(8,128)(2,1)S(1)} %get-tuple-element.97), channel_id=1, source_target_pairs={{0,16},{16,0},{32,48},{48,32},{64,80},{80,64},{96,112},{112,96},{1... | collective-permute-start | bytes 3145736 | tf_op jit(solution)/shard_map/cond/branch_0_fun/ppermute | solution.py:421
  91.3 62.8 %collective-permute-start.39 = (bf16[2048,256]{1,0:T(8,128)(2,1)S(1)}, bf16[2048,256]{1,0:T(8,128)(2,1)S(1)}, u32[]{:S(2)}, u32[]{:S(2)}) collective-permute-start(bf16[2048,256]{1,0:T(8,128)(2,1)S(1)} %get-tuple-element.98), channel_id=1, source_target_pairs={{0,16},{16,0},{32,48},{48,32},{64,80},{80,64},{96,112},{112,96},{1... | collective-permute-start | bytes 3145736 | tf_op jit(solution)/shard_map/cond/branch_0_fun/ppermute | solution.py:421
  95.1 12.6 %collective-permute-start.33 = (bf16[128,2048]{1,0:T(8,128)(2,1)S(1)}, bf16[128,2048]{1,0:T(8,128)(2,1)S(1)}, u32[]{:S(2)}, u32[]{:S(2)}) collective-permute-start(bf16[128,2048]{1,0:T(8,128)(2,1)S(1)} %pad_maximum_fusion.3), channel_id=1, source_target_pairs={{0,6},{1,7},{2,0},{3,1},{4,2},{5,3},{6,4},{7,5},{8,14},{9,15},{10,... | collective-permute-start | bytes 1572872 | tf_op jit(solution)/shard_map/cond/branch_0_fun/ppermute | solution.py:404
  98.7 12.3 %collective-permute-start.31 = (bf16[128,2048]{1,0:T(8,128)(2,1)S(1)}, bf16[128,2048]{1,0:T(8,128)(2,1)S(1)}, u32[]{:S(2)}, u32[]{:S(2)}) collective-permute-start(bf16[128,2048]{1,0:T(8,128)(2,1)S(1)} %pad_maximum_fusion.2), channel_id=1, source_target_pairs={{0,2},{1,3},{2,4},{3,5},{4,6},{5,7},{6,0},{7,1},{8,10},{9,11},{10,... | collective-permute-start | bytes 1572872 | tf_op jit(solution)/shard_map/cond/branch_0_fun/ppermute | solution.py:400
  98.8 20.1 %collective-permute-start.28 = (bf16[128,2048]{1,0:T(8,128)(2,1)S(1)}, bf16[128,2048]{1,0:T(8,128)(2,1)S(1)}, u32[]{:S(2)}, u32[]{:S(2)}) collective-permute-start(bf16[128,2048]{1,0:T(8,128)(2,1)S(1)} %pad_maximum_fusion.1), channel_id=1, source_target_pairs={{0,6},{1,7},{2,0},{3,1},{4,2},{5,3},{6,4},{7,5},{8,14},{9,15},{10,... | collective-permute-start | bytes 1572872 | tf_op jit(solution)/shard_map/cond/branch_0_fun/ppermute | solution.py:404
  107.7 13.1 %collective-permute-start.26 = (bf16[128,2048]{1,0:T(8,128)(2,1)S(1)}, bf16[128,2048]{1,0:T(8,128)(2,1)S(1)}, u32[]{:S(2)}, u32[]{:S(2)}) collective-permute-start(bf16[128,2048]{1,0:T(8,128)(2,1)S(1)} %pad_maximum_fusion), channel_id=1, source_target_pairs={{0,2},{1,3},{2,4},{3,5},{4,6},{5,7},{6,0},{7,1},{8,10},{9,11},{10,... | collective-permute-start | bytes 1572872 | tf_op jit(solution)/shard_map/cond/branch_0_fun/ppermute | solution.py:400
  111.0 29.9 %collective-permute-start.21 = (bf16[512,256]{1,0:T(8,128)(2,1)S(1)}, bf16[512,256]{1,0:T(8,128)(2,1)S(1)}, u32[]{:S(2)}, u32[]{:S(2)}) collective-permute-start(bf16[512,256]{1,0:T(8,128)(2,1)S(1)} %get-tuple-element.69), channel_id=1, source_target_pairs={{0,8},{8,0},{1,9},{9,1},{2,10},{10,2},{3,11},{11,3},{4,12},{12,4},... | collective-permute-start | bytes 786440 | tf_op jit(solution)/shard_map/cond/branch_0_fun/ppermute | solution.py:412
  118.9 27.5 %collective-permute-start.34 = (bf16[64,2048]{1,0:T(8,128)(2,1)S(1)}, bf16[64,2048]{1,0:T(8,128)(2,1)S(1)}, u32[]{:S(2)}, u32[]{:S(2)}) collective-permute-start(bf16[64,2048]{1,0:T(8,128)(2,1)S(1)} %get-tuple-element.85), channel_id=1, source_target_pairs={{0,8},{8,0},{1,9},{9,1},{2,10},{10,2},{3,11},{11,3},{4,12},{12,4},... | collective-permute-start | bytes 786440 | tf_op jit(solution)/shard_map/cond/branch_0_fun/ppermute | solution.py:412
  120.8 32.7 %collective-permute-start.35 = (bf16[64,2048]{1,0:T(8,128)(2,1)S(1)}, bf16[64,2048]{1,0:T(8,128)(2,1)S(1)}, u32[]{:S(2)}, u32[]{:S(2)}) collective-permute-start(bf16[64,2048]{1,0:T(8,128)(2,1)S(1)} %get-tuple-element.86), channel_id=1, source_target_pairs={{0,9},{1,8},{2,11},{3,10},{4,13},{5,12},{6,15},{7,14},{8,1},{9,0},... | collective-permute-start | bytes 786440 | tf_op jit(solution)/shard_map/cond/branch_0_fun/ppermute | solution.py:416
  140.9 12.6 %collective-permute-start.29 = (bf16[64,2048]{1,0:T(8,128)(2,1)S(1)}, bf16[64,2048]{1,0:T(8,128)(2,1)S(1)}, u32[]{:S(2)}, u32[]{:S(2)}) collective-permute-start(bf16[64,2048]{1,0:T(8,128)(2,1)S(1)} %get-tuple-element.79), channel_id=1, source_target_pairs={{0,1},{1,0},{2,3},{3,2},{4,5},{5,4},{6,7},{7,6},{8,9},{9,8},{10,11... | collective-permute-start | bytes 786440 | tf_op jit(solution)/shard_map/cond/branch_0_fun/ppermute | solution.py:408
  (23 other events, 179.2 us)
